TPU v7x, 768 devices: a whole 4x8x12 slice. The times are simulated.
768 devices in a mesh: row: 192 (over y, z, core), col: 4 (over x).
Axes of the slice: x: 4, y: 8, z: 12, core: 2. Of those that a mesh axis runs over, the one named last changes fastest.
Arguments:
- tiles: bfloat16 [192, 4, 64, 128, 128], P('row', 'col'), may hold values from -0.3125 to 0.3125
- tile_model: int32 [192, 4, 64], P('row', 'col'), may hold values from 0 to 1535
- ray_counts: int32 [192, 4, 16], P('row', 'col'), may hold values from 1 to 4, as said below
- data: float32 [393216], P('row'), may hold values from -40 to 40
Outputs:
- model: float32 [4, 196608], P('col', 'row')
- ray_basis: float32 [393216], P('row')
Inputs may be any that keep to these rules, and one draw needn't show every extreme that they name: `ray_counts`: each device's counts sum to at most 64; on some device every count is 4.
All inputs are finite; a program needn't handle non-finite values.
Results may differ from a plain program's by a relative error of at most 0.0051.
Values may be sent and summed in bfloat16 or wider, within the bound.
A program may use at most 32 MiB of HBM per device.

v0:
```python
import jax
import jax.numpy as jnp
from jax import lax
from jax.sharding import PartitionSpec as P

MB_DEV = 8


EPS = 1e-06
HIGH = lax.Precision.HIGHEST


def on_device(tiles, tile_model, ray_counts, data):
    tile_count = tiles.shape[2]
    edge = tiles.shape[3]
    panels = tiles.reshape(tile_count, edge, edge)
    models = tile_model.reshape(tile_count)
    counts = ray_counts.reshape(-1)
    ray_blocks = counts.shape[0]
    cumulative = jnp.cumsum(counts)
    slots = jnp.arange(tile_count, dtype=jnp.int32)
    slot_ray = jnp.sum((cumulative[None, :] <= slots[:, None]).astype(jnp.int32), axis=1)
    slot_ray = jnp.minimum(slot_ray, ray_blocks - 1)
    valid = slots < cumulative[-1]
    valid_float = valid.astype(jnp.float32)[:, None]
    ray_table = (
        (slot_ray[None, :] == jnp.arange(ray_blocks, dtype=jnp.int32)[:, None]) & valid[None, :]
    ).astype(jnp.float32)

    def left_norm(vector):
        return jnp.sqrt(lax.psum(jnp.sum(vector * vector), "row") + EPS)

    u_vec = data.reshape(ray_blocks, edge)
    beta = left_norm(u_vec)
    u_vec = u_vec / beta
    picked = u_vec.astype(jnp.bfloat16)[slot_ray]
    transposed_prod = jnp.einsum("tij,ti->tj", panels, picked, preferred_element_type=jnp.float32)
    prod = transposed_prod * valid_float
    count = MB_DEV * lax.axis_size("row")
    local_ids = models
    inside = (local_ids >= 0) & (local_ids < count)
    local_ids = jnp.where(inside, local_ids, count)
    v_vec = lax.psum_scatter(
        jax.ops.segment_sum(prod, local_ids, num_segments=count + 1)[:count],
        "row",
        scatter_dimension=0,
        tiled=True,
    )
    alpha = jnp.sqrt(lax.psum(jnp.sum(v_vec * v_vec), ("row", "col")) + EPS)
    v_vec = v_vec / alpha
    phibar = beta
    picked = lax.all_gather(v_vec.astype(jnp.bfloat16), "row", axis=0, tiled=True)[models]
    prod = jnp.einsum("tij,tj->ti", panels, picked, preferred_element_type=jnp.float32)
    partial_rays = jnp.dot(ray_table, prod, precision=HIGH)
    u_vec = lax.psum(partial_rays, "col") - alpha * u_vec
    beta = left_norm(u_vec)
    u_vec = u_vec / beta
    rho = jnp.sqrt(alpha * alpha + beta * beta)
    cosine = alpha / rho
    phi = cosine * phibar
    x_vec = phi / rho * v_vec
    model_part = x_vec.reshape(1, -1)
    return (model_part, u_vec.reshape(-1))


def solution(mesh):
    return jax.shard_map(
        on_device,
        mesh=mesh,
        in_specs=(
            P("row", "col", None, None, None),
            P("row", "col", None),
            P("row", "col", None),
            P("row"),
        ),
        out_specs=(P("col", "row"), P("row")),
        check_vma=False,
    )
```

profile of v0, /device:TPU:1, one launch (start us, length us, event | category | flops | bytes accessed | tf_op | source)
XLA Modules:
  0.0 1265.5 jit_solution(9055480117796060033)
XLA Ops:
  7.2 1.4 multiply_reduce_fusion.1
  8.7 0.7 copy.9
  9.6 0.5 slice.13
  10.1 381.7 %psum.28 = f32[]{:T(128)} all-reduce(f32[]{:T(128)} %multiply_reduce_fusion.1), channel_id=1, replica_groups=mesh['row'=192,'col'=4] {'row'}, use_global_device_ids=true, to_apply=%region_1.2 | all-reduce | flops 1 | bytes 8 | tf_op jit(solution)/shard_map/psum | solution.py:31
  392.5 0.7 convert_bitcast_fusion
  393.3 0.7 iota_compare_fusion.2
  393.9 0.7 fusion.18
  394.6 0.6 gather_fusion
  395.2 0.6 fusion.2
  395.9 1.0 scatter_custom_fusion
  396.9 1.0 slice.14
  397.9 1.3 dynamic-slice
  399.9 289.9 %all-reduce.3.cloned.1.call-done = f32[1536,128]{1,0:T(8,128)} async-done(((f32[1536,128]{1,0:T(8,128)}), f32[1536,128]{1,0:T(8,128)}) %all-reduce.3.cloned.1.call-update) | async-done | bytes 786448
  689.7 1.3 multiply_reduce_fusion.2
  691.0 106.4 %psum.29 = f32[]{:T(128)} all-reduce(f32[]{:T(128)} %multiply_reduce_fusion.2), channel_id=1, replica_groups=mesh['row'=192,'col'=4] {'row','col'}, use_global_device_ids=true, to_apply=%region_7.8 | all-reduce | flops 1 | bytes 8 | tf_op jit(solution)/shard_map/psum | solution.py:49
  798.1 0.7 fusion.15
  798.8 76.1 %all_gather.3 = bf16[1536,128]{1,0:T(8,128)(2,1)S(1)} all-gather(bf16[8,128]{1,0:T(8,128)(2,1)S(1)} %fusion.15), channel_id=1, replica_groups=mesh['row'=192,'col'=4] {'row'}, dimensions={0}, use_global_device_ids=true | all-gather | bytes 395264 | tf_op jit(solution)/shard_map/all_gather | solution.py:52
  874.9 0.6 gather_fusion.1
  875.5 1.2 fusion
  876.9 6.7 psum.30
  883.5 0.6 multiply_reduce_fusion
  884.2 371.7 %psum.31 = f32[]{:T(128)} all-reduce(f32[]{:T(128)} %multiply_reduce_fusion), channel_id=1, replica_groups=mesh['row'=192,'col'=4] {'row'}, use_global_device_ids=true, to_apply=%region_10.11 | all-reduce | flops 1 | bytes 8 | tf_op jit(solution)/shard_map/psum | solution.py:31
  1256.6 0.6 divide_bitcast_fusion
  1257.3 1.3 broadcast_multiply_fusion
  (14 shorter events, 0.5 us)
Async XLA Ops:
  7.2 388.1 %copy-start = (bf16[1,1,64,128,128]{4,3,2,1,0:T(8,128)(2,1)S(1)}, bf16[1,1,64,128,128]{4,3,2,1,0:T(8,128)(2,1)}, u32[]{:S(2)}) copy-start(bf16[1,1,64,128,128]{4,3,2,1,0:T(8,128)(2,1)} %param.4) | copy-start | bytes 6291460
  7.2 682.6 %all-reduce.3.cloned.1.call-start = ((), (), s32[]{:S(2)}) async-start(), calls=%async_computation | async-start | bytes 1572864
  397.9 485.7 %copy-start.1 = (f32[2048]{0:T(1024)S(1)}, f32[2048]{0:T(1024)}, u32[]{:S(2)}) copy-start(f32[2048]{0:T(1024)} %param.7) | copy-start | bytes 24580
Sparse Core Ops, SparseCore 0:
  398.0 291.6 all-reduce.2
where the time goes:
time: 1270 us
  blocking collectives  943 us (74%)
  waiting for transfers between devices  290 us (23%)
  between operations  17 us (1%)
    psum x2, blocking collectives, left_norm(): return jnp.sqrt(lax.psum(jnp.sum(vector * vector), 'row') + EPS)  753 us
    unnamed x2, waiting for transfers between devices  290 us
    psum x1, blocking collectives, on_device(): alpha = jnp.sqrt(lax.psum(jnp.sum(v_vec * v_vec), ('row', 'col')) + EPS)  106 us
    all_gather x1, blocking collectives, on_device(): lax.all_gather(v_vec.astype(jnp.bfloat16), 'row', axis=0, tiled=True)  76.1 us
  transfers between devices with their start and end apart: 1, of which 1 were waited for; matrix products, arithmetic and copies ran while one was open for 0% of the time, Pallas kernels for 0%

commit v1 on v0

v1 whole, which is shorter than its diff:
```python
import functools

import jax
import jax.numpy as jnp
from jax import lax
from jax.experimental import pallas as pl
from jax.experimental.pallas import tpu as pltpu
from jax.sharding import PartitionSpec as P

MESH = pl.DeviceIdType.MESH
EPS = 1e-06
F32, BF16, I32 = jnp.float32, jnp.bfloat16, jnp.int32
MB_DEV = 8
CORES = 2


def dot(a, b, contract=((1,), (0,))):
    return lax.dot_general(a, b, (contract, ((), ())), preferred_element_type=F32)


def iota(shape, axis):
    return lax.broadcasted_iota(I32, shape, axis)


def kernel(
    ny, nz, nx, slots, blocks, chunks,
    tiles_hbm, models, counts, data, model_out, ray_out,
    tiles, meta_src, meta, prod, pick, pick_t, own_sum, sib_src, sib_in, z_src, z_in,
    v_src, v_in, v_all, sel_src, sel_in, v_slots, z_sq_src, z_sq, y_sq_src, y_sq,
    x_src, x_in, fz_src, fz_in, fy_src, fy_in,
    tile_sem, s_meta, r_meta, s_prod, r_prod, s_sib, r_sib, s_z, r_z, s_v, r_v, s_va, r_va,
    s_sel, r_sel, s_zsq, r_zsq, s_ysq, r_ysq, s_x, r_x, s_fz, r_fz, s_fy, r_fy,
):
    edge = tiles.shape[-1]
    row, x = lax.axis_index("row"), lax.axis_index("col")
    c = lax.rem(row, CORES)
    z = lax.rem(row // CORES, nz)
    y = row // (CORES * nz)

    def wrap(value, size):
        return jnp.where(value >= size, value - size, value)

    def peer(dy=0, dz=0, dc=0, dx=0):
        y2, z2 = wrap(y + dy % ny, ny), wrap(z + dz % nz, nz)
        c2, x2 = wrap(c + dc, CORES), wrap(x + dx % nx, nx)
        return ((y2 * nz + z2) * CORES + c2, x2)

    def send(src, dst, s_sem, r_sem, target):
        copy = pltpu.make_async_remote_copy(
            src_ref=src, dst_ref=dst, send_sem=s_sem, recv_sem=r_sem, device_id=target, device_id_type=MESH
        )
        copy.start()
        return copy

    barrier = pltpu.get_barrier_semaphore()
    greeted = [peer(dc=1)]
    greeted += [peer(dy=d, dc=k) for d in range(1, ny) for k in range(CORES)]
    greeted += [peer(dz=d) for d in range(1, nz)]
    greeted += [peer(dx=d) for d in range(1, nx)]
    for target in greeted:
        pl.semaphore_signal(barrier, inc=1, device_id=target, device_id_type=MESH)

    step = slots // chunks
    loads = []
    for k in range(chunks):
        load = pltpu.make_async_copy(
            tiles_hbm.at[0, 0, pl.ds(k * step, step)], tiles.at[pl.ds(k * step, step)], tile_sem.at[k]
        )
        load.start()
        loads.append(load)

    count_row = counts[0].astype(F32)
    count_all = jnp.broadcast_to(count_row, (blocks, blocks))
    ahead = iota((blocks, blocks), 1) < iota((blocks, blocks), 0)
    first = jnp.sum(jnp.where(ahead, count_all, 0.0), axis=1, keepdims=True)
    upto = iota((blocks, blocks), 1) <= iota((blocks, blocks), 0)
    last = jnp.sum(jnp.where(upto, count_all, 0.0), axis=1, keepdims=True)
    first_w = jnp.broadcast_to(first, (blocks, edge))
    last_w = jnp.broadcast_to(last, (blocks, edge))
    slot_lane = iota((blocks, edge), 1).astype(F32)
    table = jnp.where((slot_lane >= first_w) & (slot_lane < last_w), 1.0, 0.0)
    used = jnp.sum(table, axis=0, keepdims=True)[:, :slots] > 0.5
    table_t = table.T[:slots].astype(BF16)

    ids = jnp.where(used, models[0].astype(F32), -1.0)
    none = jnp.full((1, edge - slots), -1.0, F32)
    d = data[...]
    d_sq = jnp.sum(d * d, axis=0, keepdims=True)
    rest = jnp.zeros((6, edge), F32)
    meta_src[0] = jnp.concatenate([jnp.concatenate([ids, none], axis=1), d_sq, rest], axis=0)
    meta_src[1] = jnp.concatenate([jnp.concatenate([none, ids], axis=1), d_sq, rest], axis=0)

    pl.semaphore_wait(barrier, len(greeted))

    sent = []
    meta_copies = [
        send(meta_src.at[k % 2], meta.at[k], s_meta.at[k], r_meta.at[k], peer(dy=k)) for k in range(1, ny)
    ]
    sent += meta_copies

    high = d.astype(BF16)
    low = (d - high.astype(F32)).astype(BF16)
    u_high, u_low = dot(table_t, high), dot(table_t, low)
    group = 8
    row_of = lax.rem(iota((2 * group, edge), 0), group)
    for k in range(chunks):
        loads[k].wait()
        for pair in range(step // (2 * group)):
            parts = []
            for half in range(2):
                base = k * step + (2 * pair + half) * group
                both = jnp.concatenate([u_high[base : base + group], u_low[base : base + group]], axis=0)
                left = jnp.concatenate(
                    [jnp.where(row_of == i, both, 0.0).astype(BF16) for i in range(group)], axis=1
                )
                right = tiles[base : base + group].reshape(group * edge, edge)
                out = dot(left, right)
                parts.append(out[:group] + out[group:])
            base = k * step + 2 * pair * group
            prod[0, base : base + 2 * group] = jnp.concatenate(parts, axis=0).astype(BF16)
    prod_copies = [
        send(prod.at[0], prod.at[k], s_prod.at[k], r_prod.at[k], peer(dy=k)) for k in range(1, ny)
    ]
    sent += prod_copies

    rows = nz * CORES * MB_DEV

    def block_of(r):
        dz = r // (CORES * MB_DEV)
        half = lax.rem(r // MB_DEV, CORES)
        z2 = wrap(dz + z, nz)
        c2 = wrap(half + c, CORES)
        return (((y * nz + z2) * CORES + c2) * MB_DEV + lax.rem(r, MB_DEV)).astype(F32)

    meta[0] = meta_src[0]
    for copy in meta_copies:
        copy.wait_recv()
    y_data_sq = meta[0, 1:2]
    for k in range(1, ny):
        y_data_sq = y_data_sq + meta[k, 1:2]
    z_sq_src[...] = jnp.broadcast_to(y_data_sq, z_sq_src.shape)
    zsq_copies = [
        send(z_sq_src, z_sq.at[k], s_zsq.at[k], r_zsq.at[k], peer(dz=k)) for k in range(1, nz)
    ]
    sent += zsq_copies
    id_rows = [jnp.maximum(meta[2 * p, 0:1], meta[2 * p + 1, 0:1]) for p in range(ny // 2)]
    block_col = block_of(iota((rows, edge), 0))
    for p in range(ny // 2):
        pick[:, p * edge : (p + 1) * edge] = jnp.where(block_col == id_rows[p], 1.0, 0.0).astype(BF16)
    id_cols = jnp.concatenate(id_rows + [none_row(edge)] * (8 - ny // 2), axis=0).T
    block_row = block_of(iota((edge, rows), 1))
    for p in range(ny // 2):
        pick_t[p * edge : (p + 1) * edge] = jnp.where(id_cols[:, p : p + 1] == block_row, 1.0, 0.0).astype(BF16)

    for copy in prod_copies:
        copy.wait_recv()
    sums = dot(pick[...], prod[...].reshape(ny * slots, edge)).reshape(nz, CORES, MB_DEV, edge)
    sib_src[...] = sums[:, 1]
    sib_copy = send(sib_src, sib_in, s_sib, r_sib, peer(dc=1))
    sent.append(sib_copy)
    own_sum[...] = sums[:, 0]
    z_data_sq = y_data_sq
    for k, copy in enumerate(zsq_copies):
        copy.wait_recv()
        z_data_sq = z_data_sq + z_sq[k + 1, 0:1]
    sib_copy.wait_recv()
    z_src[...] = own_sum[...] + sib_in[...]

    z_copies = [send(z_src.at[k], z_in.at[k], s_z.at[k], r_z.at[k], peer(dz=k)) for k in range(1, nz)]
    sent += z_copies
    v_own = z_src[0]
    for k, copy in enumerate(z_copies):
        copy.wait_recv()
        v_own = v_own + z_in[k + 1]

    v_src[0:MB_DEV] = v_own
    v_src[MB_DEV:] = jnp.broadcast_to(z_data_sq, (8, edge))
    v_copy = send(v_src, v_in, s_v, r_v, peer(dc=1))
    sent.append(v_copy)
    v_copy.wait_recv()
    data_sq = z_data_sq + v_in[MB_DEV : MB_DEV + 1]
    v_all[0] = jnp.concatenate([v_own, v_in[0:MB_DEV]], axis=0).astype(BF16)
    va_copies = [
        send(v_all.at[0], v_all.at[k], s_va.at[k], r_va.at[k], peer(dz=-k)) for k in range(1, nz)
    ]
    sent += va_copies
    for copy in va_copies:
        copy.wait_recv()
    v_y = v_all[...].reshape(rows, edge)
    sel_src[...] = dot(pick_t[...], v_y).astype(BF16).reshape(ny, slots, edge)
    sel_copies = [
        send(sel_src.at[k], sel_in.at[k], s_sel.at[k], r_sel.at[k], peer(dy=-k)) for k in range(1, ny)
    ]
    sent += sel_copies
    v_wide = v_y.astype(F32)
    y_norm = jnp.sum(v_wide * v_wide, axis=0, keepdims=True)
    y_sq_src[...] = jnp.broadcast_to(y_norm, y_sq_src.shape)
    ysq_copies = [
        send(y_sq_src, y_sq.at[k], s_ysq.at[k], r_ysq.at[k], peer(dy=k)) for k in range(1, ny)
    ]
    sent += ysq_copies
    total = sel_src[0].astype(F32)
    for k, copy in enumerate(sel_copies):
        copy.wait_recv()
        total = total + sel_in[k + 1].astype(F32)
    v_slots[...] = total

    acc = jnp.zeros((blocks, edge), F32)
    for t in range(slots):
        mine = (first_w <= float(t)) & (last_w > float(t))
        left = jnp.where(mine, jnp.broadcast_to(v_slots[t : t + 1], (blocks, edge)), 0.0).astype(BF16)
        acc = acc + dot(left, tiles[t], ((1,), (1,)))
    for k, copy in enumerate(ysq_copies):
        copy.wait_recv()
        y_norm = y_norm + y_sq[k + 1, 0:1]

    x_src[0:blocks] = acc
    x_src[blocks:] = jnp.broadcast_to(y_norm, (8, edge))
    x_copies = [send(x_src, x_in.at[k], s_x.at[k], r_x.at[k], peer(dx=k)) for k in range(1, nx)]
    sent += x_copies
    full = x_src[...]
    for k, copy in enumerate(x_copies):
        copy.wait_recv()
        full = full + x_in[k + 1]
    beta0 = jnp.sqrt(jnp.sum(data_sq, axis=1, keepdims=True) + EPS)
    v_sq = jnp.sum(full[blocks : blocks + 1], axis=1, keepdims=True)
    alpha = jnp.sqrt(v_sq / (beta0 * beta0) + EPS)
    u = full[0:blocks] * (1.0 / beta0 / alpha) - d * (alpha / beta0)
    part = jnp.sum(u * u, axis=0, keepdims=True)

    fz_src[...] = jnp.broadcast_to(part, fz_src.shape)
    fz_copies = [send(fz_src, fz_in.at[k], s_fz.at[k], r_fz.at[k], peer(dz=k)) for k in range(1, nz)]
    sent += fz_copies
    for k, copy in enumerate(fz_copies):
        copy.wait_recv()
        part = part + fz_in[k + 1, 0:1]
    fy_src[...] = jnp.broadcast_to(part, fy_src.shape)
    fy_copies = []
    for k in range(1, ny * CORES):
        fy_copies.append(
            send(fy_src, fy_in.at[k], s_fy.at[k], r_fy.at[k], peer(dy=k // CORES, dc=k % CORES))
        )
    sent += fy_copies
    for k, copy in enumerate(fy_copies):
        copy.wait_recv()
        part = part + fy_in[k + 1, 0:1]
    beta_sq = jnp.sum(part, axis=1, keepdims=True) + EPS
    ray_out[...] = u * (1.0 / jnp.sqrt(beta_sq))
    model_out[...] = v_own * (1.0 / (alpha * alpha + beta_sq))
    for copy in sent:
        copy.wait_send()


def none_row(edge):
    return jnp.full((1, edge), -1.0, F32)


def build(mesh, ny, nz, nx):
    def on_device(tiles, tile_model, ray_counts, data):
        slots, edge = tiles.shape[2], tiles.shape[3]
        blocks = ray_counts.shape[2]
        chunks = 4
        rows = nz * CORES * MB_DEV
        vmem, dma = pltpu.VMEM, pltpu.SemaphoreType.DMA
        model, rays = pl.pallas_call(
            functools.partial(kernel, ny, nz, nx, slots, blocks, chunks),
            out_shape=(
                jax.ShapeDtypeStruct((MB_DEV, edge), F32),
                jax.ShapeDtypeStruct((blocks, edge), F32),
            ),
            in_specs=[
                pl.BlockSpec(memory_space=pltpu.HBM),
                pl.BlockSpec(memory_space=pltpu.VMEM),
                pl.BlockSpec(memory_space=pltpu.VMEM),
                pl.BlockSpec(memory_space=pltpu.VMEM),
            ],
            out_specs=(pl.BlockSpec(memory_space=pltpu.VMEM), pl.BlockSpec(memory_space=pltpu.VMEM)),
            scratch_shapes=[
                vmem((slots, edge, edge), BF16),
                vmem((2, 8, edge), F32),
                vmem((ny, 8, edge), F32),
                vmem((ny, slots, edge), BF16),
                vmem((rows, ny * slots), BF16),
                vmem((ny * slots, rows), BF16),
                vmem((nz, MB_DEV, edge), F32),
                vmem((nz, MB_DEV, edge), F32),
                vmem((nz, MB_DEV, edge), F32),
                vmem((nz, MB_DEV, edge), F32),
                vmem((nz, MB_DEV, edge), F32),
                vmem((2 * MB_DEV, edge), F32),
                vmem((2 * MB_DEV, edge), F32),
                vmem((nz, 2 * MB_DEV, edge), BF16),
                vmem((ny, slots, edge), BF16),
                vmem((ny, slots, edge), BF16),
                vmem((slots, edge), F32),
                vmem((8, edge), F32),
                vmem((nz, 8, edge), F32),
                vmem((8, edge), F32),
                vmem((ny, 8, edge), F32),
                vmem((blocks + 8, edge), F32),
                vmem((nx, blocks + 8, edge), F32),
                vmem((8, edge), F32),
                vmem((nz, 8, edge), F32),
                vmem((8, edge), F32),
                vmem((ny * CORES, 8, edge), F32),
                dma((chunks,)),
                dma((ny,)), dma((ny,)),
                dma((ny,)), dma((ny,)),
                dma, dma,
                dma((nz,)), dma((nz,)),
                dma, dma,
                dma((nz,)), dma((nz,)),
                dma((ny,)), dma((ny,)),
                dma((nz,)), dma((nz,)),
                dma((ny,)), dma((ny,)),
                dma((nx,)), dma((nx,)),
                dma((nz,)), dma((nz,)),
                dma((ny * CORES,)), dma((ny * CORES,)),
            ],
            compiler_params=pltpu.CompilerParams(
                collective_id=0, has_side_effects=True, vmem_limit_bytes=32 * 1024 * 1024
            ),
        )(tiles, tile_model, ray_counts, data.reshape(blocks, edge))
        return model.reshape(1, -1), rays.reshape(-1)

    return jax.shard_map(
        on_device,
        mesh=mesh,
        in_specs=(
            P("row", "col", None, None, None),
            P("row", "col", None),
            P("row", "col", None),
            P("row"),
        ),
        out_specs=(P("col", "row"), P("row")),
        check_vma=False,
    )


def solution(mesh):
    nz = 12
    return build(mesh, mesh.shape["row"] // (CORES * nz), nz, mesh.shape["col"])
```

time: 1270 us -> 74.4 us (0.06)
  blocking collectives: 943 us -> 0 us
  waiting for transfers between devices: 290 us -> 0 us
  Pallas kernels: 0 us -> 68.7 us
  between operations: 17 us -> 0.65 us
    psum x4 -> x0, blocking collectives: 866 us -> none  [the longest x2 753 us: left_norm(): return jnp.sqrt(lax.psum(jnp.sum(vector * vector), 'row') + EPS)]
    unnamed x2 -> x0, waiting for transfers between devices: 290 us -> none
    all_gather x1 -> x0, blocking collectives: 76.1 us -> none  [on_device(): lax.all_gather(v_vec.astype(jnp.bfloat16), 'row', axis=0, tiled=True)]
    pallas_call x0 -> x1, Pallas kernels: none -> 68.7 us  [on_device(): pl.pallas_call(functools.partial(kernel, ny, nz, nx, slots, blocks, chunk...]
  transfers between devices with their start and end apart: 1 -> 0, of which waited for: 1 -> 0; matrix products, arithmetic and copies ran while one was open for 0% -> 0% of each run, Pallas kernels for 0% -> 0%
where the time goes in v1:
time: 74.4 us; the launch traced here: 74.1 us
  Pallas kernels  68.7 us (92%)
  local copies, waits for them, and re-layouts  4.78 us (6%)
    pallas_call x1, Pallas kernels, on_device(): pl.pallas_call(functools.partial(kernel, ny, nz, nx, slots, blocks, chunk...  68.7 us
    unnamed x10, local copies, waits for them, and re-layouts  4.78 us

profile of v1, /device:TPU:1, one launch (start us, length us, event | category | flops | bytes accessed | tf_op | source)
XLA Modules:
  0.0 74.1 jit_solution(5231359512341122844)
XLA Ops:
  0.6 0.0 copy-start
  0.6 1.6 %copy-done = bf16[1,1,64,128,128]{4,3,2,1,0:T(8,128)(2,1)S(1)} copy-done((bf16[1,1,64,128,128]{4,3,2,1,0:T(8,128)(2,1)S(1)}, bf16[1,1,64,128,128]{4,3,2,1,0:T(8,128)(2,1)}, u32[]{:S(2)}) %copy-start) | copy-done | bytes 2097176
  2.2 0.0 copy-start.1
  2.2 0.7 copy-done.1
  2.9 0.0 copy-start.2
  2.9 0.7 copy-done.2
  3.6 0.0 copy-start.3
  3.6 0.7 copy-done.3
  4.2 68.7 %shard_map.59 = (f32[8,128]{1,0:T(8,128)S(1)}, f32[16,128]{1,0:T(8,128)S(1)}) custom-call(bf16[1,1,64,128,128]{4,3,2,1,0:T(8,128)(2,1)S(1)} %copy-done, s32[1,1,64]{2,1,0:T(1,128)S(1)} %copy-done.2, s32[1,1,16]{2,1,0:T(1,128)S(1)} %copy-done.3, f32[16,128]{1,0:T(8,128)S(1)} %bitcast.3), custom_call_target="tpu_custom_call" | custom-call | tf_op jit(solution)/shard_map/pallas_call | solution.py:265
  72.9 0.6 copy.8
  73.5 0.6 copy.9
Async XLA Ops:
  0.6 1.6 %copy-start = (bf16[1,1,64,128,128]{4,3,2,1,0:T(8,128)(2,1)S(1)}, bf16[1,1,64,128,128]{4,3,2,1,0:T(8,128)(2,1)}, u32[]{:S(2)}) copy-start(bf16[1,1,64,128,128]{4,3,2,1,0:T(8,128)(2,1)} %tiles_hbm.1) | copy-start | bytes 6291460
  2.2 0.7 copy-start.1
  2.9 0.7 copy-start.2
  3.6 0.7 copy-start.3

commit v2 on v1

v2 whole, which is shorter than its diff:
```python
import functools

import jax
import jax.numpy as jnp
from jax import lax
from jax.experimental import pallas as pl
from jax.experimental.pallas import tpu as pltpu
from jax.sharding import PartitionSpec as P

MESH = pl.DeviceIdType.MESH
EPS = 1e-06
F32, BF16, I32 = jnp.float32, jnp.bfloat16, jnp.int32
MB_DEV = 8
CORES = 2


def dot(a, b, contract=((1,), (0,))):
    return lax.dot_general(a, b, (contract, ((), ())), preferred_element_type=F32)


def iota(shape, axis):
    return lax.broadcasted_iota(I32, shape, axis)


def kernel(
    ny, nz, nx, slots, blocks, chunks, wide,
    tiles_hbm, models_hbm, counts_hbm, data_hbm, model_out, ray_out,
    tiles, models, counts, data, give_src, give, ask_src, ask, prod, match, picked,
    sel_src, sel_in, v_slots, x_src, x_in, f_in,
    tile_sem, in_sem, s_give, r_give, s_ask, r_ask, s_prod, r_prod, s_rel, r_rel,
    s_sel, r_sel, s_x, r_x, s_f, r_f,
):
    edge = tiles.shape[-1]
    row, x = lax.axis_index("row"), lax.axis_index("col")
    c = lax.rem(row, CORES)
    z = lax.rem(row // CORES, nz)
    y = row // (CORES * nz)

    def wrap(value, size):
        return jnp.where(value >= size, value - size, value)

    def peer(dy=0, dz=0, dc=0, dx=0):
        y2, z2 = wrap(y + dy % ny, ny), wrap(z + dz % nz, nz)
        c2, x2 = wrap(c + dc, CORES), wrap(x + dx % nx, nx)
        return ((y2 * nz + z2) * CORES + c2, x2)

    def far(size):
        return sorted(range(1, size), key=lambda k: -min(k, size - k))

    def send(src, dst, s_sem, r_sem, target):
        copy = pltpu.make_async_remote_copy(
            src_ref=src, dst_ref=dst, send_sem=s_sem, recv_sem=r_sem, device_id=target, device_id_type=MESH
        )
        copy.start()
        return copy

    barrier = pltpu.get_barrier_semaphore()
    greeted = [peer(dc=1)]
    greeted += [peer(dy=d) for d in range(1, ny)]
    greeted += [peer(dz=d, dc=k) for d in range(1, nz) for k in range(CORES)]
    greeted += [peer(dx=d, dc=k) for d in range(1, nx) for k in range(CORES)]
    for target in greeted:
        pl.semaphore_signal(barrier, inc=1, device_id=target, device_id_type=MESH)

    small = []
    for k, (src, dst) in enumerate(((counts_hbm, counts), (models_hbm, models), (data_hbm, data))):
        load = pltpu.make_async_copy(src, dst, in_sem.at[k])
        load.start()
        small.append(load)
    step = slots // chunks
    loads = []
    for k in range(chunks):
        load = pltpu.make_async_copy(
            tiles_hbm.at[0, 0, pl.ds(k * step, step)], tiles.at[pl.ds(k * step, step)], tile_sem.at[k]
        )
        load.start()
        loads.append(load)

    for load in small:
        load.wait()

    count_row = counts[0].astype(F32)
    count_all = jnp.broadcast_to(count_row, (blocks, blocks))
    ahead = iota((blocks, blocks), 1) < iota((blocks, blocks), 0)
    first = jnp.sum(jnp.where(ahead, count_all, 0.0), axis=1, keepdims=True)
    upto = iota((blocks, blocks), 1) <= iota((blocks, blocks), 0)
    last = jnp.sum(jnp.where(upto, count_all, 0.0), axis=1, keepdims=True)
    first_w = jnp.broadcast_to(first, (blocks, edge))
    last_w = jnp.broadcast_to(last, (blocks, edge))
    slot_lane = iota((blocks, edge), 1).astype(F32)
    table = jnp.where((slot_lane >= first_w) & (slot_lane < last_w), 1.0, 0.0)
    used = jnp.sum(table, axis=0, keepdims=True)[:, :slots] > 0.5
    table_t = table.T[:slots].astype(BF16)

    models_row = models[0].astype(F32)
    ids = jnp.where(used, models_row, -1.0)
    none = jnp.full((1, edge - slots), -1.0, F32)
    give_src[0:1] = jnp.concatenate([ids, none], axis=1)
    give_src[8:9] = jnp.concatenate([none, ids], axis=1)
    lane = iota((1, edge), 1)
    owned = jnp.where(lane < slots + MB_DEV, (row * MB_DEV + lane - slots).astype(F32), -2.0)
    asked = jnp.concatenate([jnp.where(used, models_row, -2.0), none], axis=1)
    ask_src[0:1] = jnp.where(lane < slots, asked, owned)
    d = data[...]

    high = d.astype(BF16)
    low = (d - high.astype(F32)).astype(BF16)
    u_high, u_low = dot(table_t, high), dot(table_t, low)
    group = 8
    row_of = lax.rem(iota((2 * group, edge), 0), group)
    for k in range(chunks):
        loads[k].wait()
        for pair in range(step // (2 * group)):
            parts = []
            for half in range(2):
                base = k * step + (2 * pair + half) * group
                both = jnp.concatenate([u_high[base : base + group], u_low[base : base + group]], axis=0)
                left = jnp.concatenate(
                    [jnp.where(row_of == i, both, 0.0).astype(BF16) for i in range(group)], axis=1
                )
                right = tiles[base : base + group].reshape(group * edge, edge)
                out = dot(left, right)
                parts.append(out[:group] + out[group:])
            base = k * step + 2 * pair * group
            prod[0, 0, 0, base : base + 2 * group] = jnp.concatenate(parts, axis=0).astype(BF16)

    order = [0] + [k for i in range(1, nz // 2 + 1) for k in ((i, nz - i) if 2 * i != nz else (i,))]
    place = {k: (order.index(k) // 2, order.index(k) % 2) for k in order}
    sent = []
    pl.semaphore_wait(barrier, len(greeted))
    ask_copies = [
        send(ask_src.at[0:1], ask.at[k : k + 1], s_ask.at[k], r_ask.at[k], peer(dy=k)) for k in far(ny)
    ]
    give_copies = []
    for k in far(nz) + [0]:
        for i in range(CORES):
            if k + i > 0:
                half, slot = 8 * place[k][1], i * nz + k
                give_copies.append(
                    send(
                        give_src.at[half : half + 1], give.at[slot : slot + 1],
                        s_give.at[slot], r_give.at[slot], peer(dz=k, dc=i),
                    )
                )
    prod_copies = {
        k: send(
            prod.at[0, 0, 0], prod.at[place[k][0], 0, place[k][1]], s_prod.at[k], r_prod.at[k], peer(dz=k)
        )
        for k in far(nz)
    }

    def relay(k):
        pair, j = place[k]
        return send(prod.at[pair, 0, j], prod.at[pair, 1, j], s_rel.at[k], r_rel.at[k], peer(dc=1))

    relays = {0: relay(0)}
    sent += ask_copies + give_copies + list(prod_copies.values())

    for copy in ask_copies:
        copy.wait_recv()
    ask[0:1] = ask_src[0:1]
    ask_cols = ask[...].T
    for copy in give_copies:
        copy.wait_recv()
    give[0:1] = give_src[0:1]
    for pair in range(nz // 2):
        for i in range(CORES):
            k0, k1 = i * nz + order[2 * pair], i * nz + order[2 * pair + 1]
            given = jnp.maximum(give[k0 : k0 + 1], give[k1 : k1 + 1])
            for p in range(ny):
                wanted = jnp.broadcast_to(ask_cols[0:wide, p : p + 1], (wide, edge))
                match[pair, p * wide : (p + 1) * wide, i * edge : (i + 1) * edge] = jnp.where(
                    wanted == given, 1.0, 0.0
                ).astype(BF16)

    def add(pair):
        for j in range(2):
            relays[order[2 * pair + j]].wait_recv()
        part = dot(match[pair], prod[pair].reshape(CORES * 2 * slots, edge))
        picked[...] = part if pair == 0 else picked[...] + part

    for pair in range(nz // 2):
        for j in range(2):
            k = order[2 * pair + j]
            if k > 0:
                prod_copies[k].wait_recv()
                relays[k] = relay(k)
        if pair > 0:
            add(pair - 1)
    add(nz // 2 - 1)
    sent += list(relays.values())

    sel_src[...] = picked[...].astype(BF16).reshape(ny, wide, edge)
    sel_copies = [
        send(sel_src.at[k], sel_in.at[k], s_sel.at[k], r_sel.at[k], peer(dy=-k)) for k in far(ny)
    ]
    sent += sel_copies
    total = picked[0:wide].astype(BF16).astype(F32)
    for copy in sel_copies:
        copy.wait_recv()
    for k in range(1, ny):
        total = total + sel_in[k].astype(F32)
    v_own = total[slots : slots + MB_DEV]
    v_slots[...] = total[0:slots]

    acc = jnp.zeros((blocks, edge), F32)
    for t in range(slots):
        mine = (first_w <= float(t)) & (last_w > float(t))
        left = jnp.where(mine, jnp.broadcast_to(v_slots[t : t + 1], (blocks, edge)), 0.0).astype(BF16)
        acc = acc + dot(left, tiles[t], ((1,), (1,)))

    def over_rows(value):
        return jnp.sum(value, axis=0, keepdims=True)

    x_src[0:blocks] = acc
    terms = [over_rows(v_own * v_own), over_rows(acc * d), over_rows(d * d)]
    x_src[blocks:] = jnp.concatenate(terms + [jnp.zeros((8 - len(terms), edge), F32)], axis=0)
    rows = pl.ds(0, blocks + len(terms))
    x_copies = [
        send(x_src.at[rows], x_in.at[nx * i + k, rows], s_x.at[nx * i + k], r_x.at[nx * i + k], peer(dx=k, dc=i))
        for k in far(nx) + [0]
        for i in range(CORES)
        if k + i > 0
    ]
    sent += x_copies
    for copy in x_copies:
        copy.wait_recv()
    own, other = x_src[0 : blocks + 2], x_in[nx, 0 : blocks + 2]
    for k in range(1, nx):
        own = own + x_in[k, 0 : blocks + 2]
        other = other + x_in[nx + k, 0 : blocks + 2]
    g = own[0:blocks]
    g_other = other[0:blocks]
    v_row = own[blocks : blocks + 1] + other[blocks : blocks + 1]
    gd_row = own[blocks + 1 : blocks + 2] + other[blocks + 1 : blocks + 2]
    d_row = x_src[blocks + 2 : blocks + 3] + x_in[nx, blocks + 2 : blocks + 3]
    g_row = over_rows(g * g + g_other * g_other)

    quarter = edge // 4
    stack = jnp.concatenate([g_row, gd_row, d_row, v_row, jnp.zeros((4, edge), F32)], axis=0)
    stack = stack + pltpu.roll(stack, 2 * quarter, 1)
    stack = stack + pltpu.roll(stack, quarter, 1)
    mine = iota((8, edge), 1) // quarter == iota((8, edge), 0)
    f_in[0:1] = over_rows(jnp.where(mine, stack, 0.0))
    f_copies = []
    for i in far(ny) + [0]:
        for k in far(nz) + [0]:
            slot = i * nz + k
            if slot > 0:
                f_copies.append(
                    send(f_in.at[0:1], f_in.at[slot : slot + 1], s_f.at[slot], r_f.at[slot], peer(dy=i, dz=k))
                )
    sent += f_copies
    for copy in f_copies:
        copy.wait_recv()
    sums = jnp.broadcast_to(over_rows(f_in[...]), (8, edge))
    sums = jnp.sum(jnp.where(mine, sums, 0.0), axis=1, keepdims=True)
    g_sq, gd, d_sq, v_sq = sums[0:1], sums[1:2], sums[2:3], sums[3:4]
    beta0_sq = d_sq + EPS
    beta0 = jnp.sqrt(beta0_sq)
    alpha_sq = v_sq / beta0_sq + EPS
    alpha = jnp.sqrt(alpha_sq)
    scale = 1.0 / (beta0 * alpha)
    u_sq = g_sq * (scale * scale) - (2.0 / beta0_sq) * gd + (alpha_sq / beta0_sq) * d_sq
    beta_sq = jnp.maximum(u_sq, 0.0) + EPS
    back = 1.0 / jnp.sqrt(beta_sq)
    ray_out[...] = g * (scale * back) - d * (alpha / beta0 * back)
    model_out[...] = v_own * (1.0 / (alpha_sq + beta_sq))
    for copy in sent:
        copy.wait_send()


def build(mesh, ny, nz, nx):
    def on_device(tiles, tile_model, ray_counts, data):
        slots, edge = tiles.shape[2], tiles.shape[3]
        blocks = ray_counts.shape[2]
        chunks = 4
        wide = slots + 16
        rows = ny * wide
        vmem, dma = pltpu.VMEM, pltpu.SemaphoreType.DMA
        model, rays = pl.pallas_call(
            functools.partial(kernel, ny, nz, nx, slots, blocks, chunks, wide),
            out_shape=(
                jax.ShapeDtypeStruct((MB_DEV, edge), F32),
                jax.ShapeDtypeStruct((blocks, edge), F32),
            ),
            in_specs=[
                pl.BlockSpec(memory_space=pl.ANY),
                pl.BlockSpec(memory_space=pl.ANY),
                pl.BlockSpec(memory_space=pl.ANY),
                pl.BlockSpec(memory_space=pl.ANY),
            ],
            out_specs=(pl.BlockSpec(memory_space=pltpu.VMEM), pl.BlockSpec(memory_space=pltpu.VMEM)),
            scratch_shapes=[
                vmem((slots, edge, edge), BF16),
                vmem(tile_model.shape, I32),
                vmem(ray_counts.shape, I32),
                vmem((blocks, edge), F32),
                vmem((16, edge), F32),
                vmem((CORES * nz, edge), F32),
                vmem((8, edge), F32),
                vmem((ny, edge), F32),
                vmem((nz // 2, CORES, 2, slots, edge), BF16),
                vmem((nz // 2, rows, CORES * 2 * slots), BF16),
                vmem((rows, edge), F32),
                vmem((ny, wide, edge), BF16),
                vmem((ny, wide, edge), BF16),
                vmem((slots, edge), F32),
                vmem((blocks + 8, edge), F32),
                vmem((CORES * nx, blocks + 8, edge), F32),
                vmem((ny * nz, edge), F32),
                dma((chunks,)), dma((3,)),
                dma((CORES * nz,)), dma((CORES * nz,)),
                dma((ny,)), dma((ny,)),
                dma((nz,)), dma((nz,)),
                dma((nz,)), dma((nz,)),
                dma((ny,)), dma((ny,)),
                dma((CORES * nx,)), dma((CORES * nx,)),
                dma((ny * nz,)), dma((ny * nz,)),
            ],
            compiler_params=pltpu.CompilerParams(
                collective_id=0, has_side_effects=True, vmem_limit_bytes=56 * 1024 * 1024
            ),
        )(tiles, tile_model, ray_counts, data.reshape(blocks, edge))
        return model.reshape(1, -1), rays.reshape(-1)

    return jax.shard_map(
        on_device,
        mesh=mesh,
        in_specs=(
            P("row", "col", None, None, None),
            P("row", "col", None),
            P("row", "col", None),
            P("row"),
        ),
        out_specs=(P("col", "row"), P("row")),
        check_vma=False,
    )


def solution(mesh):
    nz = 12
    return build(mesh, mesh.shape["row"] // (CORES * nz), nz, mesh.shape["col"])
```

time: 74.4 us -> 59.2 us (0.80)
  Pallas kernels: 68.7 us -> 55.8 us
  local copies, waits for them, and re-layouts: 4.78 us -> 2.56 us
    pallas_call x1, Pallas kernels: 68.7 us -> 55.8 us  [on_device(): pl.pallas_call(functools.partial(kernel, ny, nz, nx, slots, blocks, chunk...]
    unnamed x10 -> x2, local copies, waits for them, and re-layouts: 4.78 us -> 2.56 us
where the time goes in v2:
time: 59.2 us; the launch traced here: 59 us
  Pallas kernels  55.8 us (94%)
  local copies, waits for them, and re-layouts  2.56 us (4%)
  between operations  0.64 us (1%)
    pallas_call x1, Pallas kernels, on_device(): pl.pallas_call(functools.partial(kernel, ny, nz, nx, slots, blocks, chunk...  55.8 us
    unnamed x2, local copies, waits for them, and re-layouts  2.56 us

profile of v2, /device:TPU:1, one launch (start us, length us, event | category | flops | bytes accessed | tf_op | source)
XLA Modules:
  0.0 59.0 jit_solution(16218170061771592829)
XLA Ops:
  0.6 55.8 %shard_map.59 = (f32[8,128]{1,0:T(8,128)}, f32[16,128]{1,0:T(8,128)}) custom-call(bf16[1,1,64,128,128]{4,3,2,1,0:T(8,128)(2,1)} %tiles_hbm.1, s32[1,1,64]{2,1,0:T(1,128)} %models_hbm.1, s32[1,1,16]{2,1,0:T(1,128)} %counts_hbm.1, f32[16,128]{1,0:T(8,128)} %bitcast.3), custom_call_target="tpu_custom_call" | custom-call | tf_op jit(solution)/shard_map/pallas_call | solution.py:281
  56.4 1.3 %copy.8 = f32[1,1024]{1,0:T(1,128)} copy(f32[1,1024]{1,0:T(1,128)} %bitcast.5) | data formatting | bytes 8192
  57.7 1.3 %copy.9 = f32[2048]{0:T(1024)} copy(f32[2048]{0:T(1024)} %bitcast.4) | data formatting | bytes 16384

commit v3 on v2

v3 whole, which is shorter than its diff:
```python
import functools

import jax
import jax.numpy as jnp
from jax import lax
from jax.experimental import pallas as pl
from jax.experimental.pallas import tpu as pltpu
from jax.sharding import PartitionSpec as P

MESH = pl.DeviceIdType.MESH
EPS = 1e-06
F32, BF16, I32 = jnp.float32, jnp.bfloat16, jnp.int32
MB_DEV = 8
CORES = 2


def dot(a, b, contract=((1,), (0,))):
    return lax.dot_general(a, b, (contract, ((), ())), preferred_element_type=F32)


def iota(shape, axis):
    return lax.broadcasted_iota(I32, shape, axis)


def kernel(
    ny, nz, nx, slots, blocks, chunks, wide,
    tiles_hbm, integers, data_hbm, model_out, ray_out,
    tiles, data, give_src, give, ask_src, ask, prod, match, picked,
    sel_src, sel_in, v_slots, x_src, x_in, f_in,
    tile_sem, in_sem, s_give, r_give, s_ask, r_ask, s_prod, r_prod, s_rel, r_rel,
    s_sel, r_sel, s_own, r_own, s_x, r_x, s_f, r_f,
):
    edge = tiles.shape[-1]
    row, x = lax.axis_index("row"), lax.axis_index("col")
    c = lax.rem(row, CORES)
    z = lax.rem(row // CORES, nz)
    y = row // (CORES * nz)

    def wrap(value, size):
        return jnp.where(value >= size, value - size, value)

    def peer(dy=0, dz=0, dc=0, dx=0):
        y2, z2 = wrap(y + dy % ny, ny), wrap(z + dz % nz, nz)
        c2, x2 = wrap(c + dc, CORES), wrap(x + dx % nx, nx)
        return ((y2 * nz + z2) * CORES + c2, x2)

    def far(size):
        return sorted(range(1, size), key=lambda k: -min(k, size - k))

    def send(src, dst, s_sem, r_sem, target):
        copy = pltpu.make_async_remote_copy(
            src_ref=src, dst_ref=dst, send_sem=s_sem, recv_sem=r_sem, device_id=target, device_id_type=MESH
        )
        copy.start()
        return copy

    data_load = pltpu.make_async_copy(data_hbm, data, in_sem)
    data_load.start()
    step = slots // chunks
    loads = []
    for k in range(chunks):
        load = pltpu.make_async_copy(
            tiles_hbm.at[0, 0, pl.ds(k * step, step)], tiles.at[pl.ds(k * step, step)], tile_sem.at[k]
        )
        load.start()
        loads.append(load)

    def group(ref, s_sem, r_sem):
        return pltpu.make_async_remote_copy(
            src_ref=ref, dst_ref=ref, send_sem=s_sem, recv_sem=r_sem, device_id=peer(dc=1), device_id_type=MESH
        )

    barrier = pltpu.get_barrier_semaphore()
    greeted = [peer(dz=d, dc=k) for d in far(nz) for k in range(CORES)]
    greeted += [peer(dy=d) for d in far(ny)]
    greeted += [peer(dx=d, dc=k) for d in far(nx) for k in range(CORES)]
    greeted += [peer(dc=1)]
    for target in greeted:
        pl.semaphore_signal(barrier, inc=1, device_id=target, device_id_type=MESH)

    count_row = integers[0].astype(F32)[:, slots : slots + blocks]
    count_all = jnp.broadcast_to(count_row, (blocks, blocks))
    ahead = iota((blocks, blocks), 1) < iota((blocks, blocks), 0)
    first = jnp.sum(jnp.where(ahead, count_all, 0.0), axis=1, keepdims=True)
    upto = iota((blocks, blocks), 1) <= iota((blocks, blocks), 0)
    last = jnp.sum(jnp.where(upto, count_all, 0.0), axis=1, keepdims=True)
    first_w = jnp.broadcast_to(first, (blocks, edge))
    last_w = jnp.broadcast_to(last, (blocks, edge))
    slot_lane = iota((blocks, edge), 1).astype(F32)
    table = jnp.where((slot_lane >= first_w) & (slot_lane < last_w), 1.0, 0.0)
    used = jnp.sum(table, axis=0, keepdims=True)[:, :slots] > 0.5
    table_t = table.T[:slots].astype(BF16)

    models_row = integers[0].astype(F32)[:, 0:slots]
    ids = jnp.where(used, models_row, -1.0)
    none = jnp.full((1, edge - slots), -1.0, F32)
    give_src[0:1] = jnp.concatenate([ids, none], axis=1)
    give_src[8:9] = jnp.concatenate([none, ids], axis=1)
    lane = iota((1, edge), 1)
    owned = jnp.where(lane < slots + MB_DEV, (row * MB_DEV + lane - slots).astype(F32), -2.0)
    asked = jnp.concatenate([jnp.where(used, models_row, -2.0), none], axis=1)
    ask_src[0:1] = jnp.where(lane < slots, asked, owned)
    data_load.wait()
    d = data[...]

    order = far(nz) + [0]
    place = {k: (order.index(k) // 2, order.index(k) % 2) for k in order}
    home = prod.at[place[0][0], 0, place[0][1]]

    high = d.astype(BF16)
    low = (d - high.astype(F32)).astype(BF16)
    u_high, u_low = dot(table_t, high), dot(table_t, low)
    eight = 8
    row_of = lax.rem(iota((2 * eight, edge), 0), eight)
    for k in range(chunks):
        loads[k].wait()
        for pair in range(step // (2 * eight)):
            parts = []
            for half in range(2):
                base = k * step + (2 * pair + half) * eight
                both = jnp.concatenate([u_high[base : base + eight], u_low[base : base + eight]], axis=0)
                left = jnp.concatenate(
                    [jnp.where(row_of == i, both, 0.0).astype(BF16) for i in range(eight)], axis=1
                )
                right = tiles[base : base + eight].reshape(eight * edge, edge)
                out = dot(left, right)
                parts.append(out[:eight] + out[eight:])
            base = k * step + 2 * pair * eight
            home[base : base + 2 * eight] = jnp.concatenate(parts, axis=0).astype(BF16)

    sent = []
    pl.semaphore_wait(barrier, len(greeted))
    for k in far(ny):
        send(ask_src.at[0:1], ask.at[k : k + 1], s_ask, r_ask, peer(dy=k))
    for k in far(nz) + [0]:
        for i in range(CORES):
            if k + i > 0:
                half, slot = 8 * place[k][1], i * nz + k
                send(
                    give_src.at[half : half + 1], give.at[slot : slot + 1], s_give, r_give, peer(dz=k, dc=i)
                )
    for k in far(nz):
        pair, j = place[k]
        send(home, prod.at[pair, 0, j], s_prod.at[pair], r_prod.at[pair], peer(dz=k))
    prods = [
        group(prod.at[pair, 0] if 2 * pair + 2 < nz else prod.at[pair, 0, 0], s_prod.at[pair], r_prod.at[pair])
        for pair in range(nz // 2)
    ]
    asks = group(ask.at[1:ny], s_ask, r_ask)
    gives = group(give.at[1 : CORES * nz], s_give, r_give)
    relays = [group(prod.at[pair, 1], s_rel, r_rel.at[pair]) for pair in range(nz // 2)]
    relayed = group(prod.at[:, 0], s_rel, r_rel.at[0])

    def relay(k):
        pair, j = place[k]
        send(prod.at[pair, 0, j], prod.at[pair, 1, j], s_rel, r_rel.at[pair], peer(dc=1))

    relay(0)
    sent += [asks, gives, relayed] + prods

    asks.wait_recv()
    ask[0:1] = ask_src[0:1]
    ask_cols = ask[...].T
    gives.wait_recv()
    half = 8 * place[0][1]
    give[0:1] = give_src[half : half + 1]
    for pair in range(nz // 2):
        for i in range(CORES):
            k0, k1 = i * nz + order[2 * pair], i * nz + order[2 * pair + 1]
            given = jnp.maximum(give[k0 : k0 + 1], give[k1 : k1 + 1])
            for p in range(ny):
                wanted = jnp.broadcast_to(ask_cols[0:wide, p : p + 1], (wide, edge))
                match[pair, p * wide : (p + 1) * wide, i * edge : (i + 1) * edge] = jnp.where(
                    wanted == given, 1.0, 0.0
                ).astype(BF16)

    def add(pair):
        relays[pair].wait_recv()
        part = dot(match[pair], prod[pair].reshape(CORES * 2 * slots, edge))
        picked[...] = part if pair == 0 else picked[...] + part

    for pair in range(nz // 2):
        prods[pair].wait_recv()
        for k in order[2 * pair : 2 * pair + 2]:
            if k > 0:
                relay(k)
        if pair > 0:
            add(pair - 1)
    add(nz // 2 - 1)

    sel_src[...] = picked[...].astype(BF16).reshape(ny, wide, edge)
    slot_rows, own_rows = pl.ds(0, slots), pl.ds(slots, wide - slots)
    for k in far(ny):
        send(sel_src.at[k, slot_rows], sel_in.at[k, slot_rows], s_sel, r_sel, peer(dy=-k))
    for k in far(ny):
        send(sel_src.at[k, own_rows], sel_in.at[k, own_rows], s_own, r_own, peer(dy=-k))
    sels = group(sel_in.at[1:ny, slot_rows], s_sel, r_sel)
    owns = group(sel_in.at[1:ny, own_rows], s_own, r_own)
    sent += [sels, owns]
    total = picked[0:slots].astype(BF16).astype(F32)
    sels.wait_recv()
    for k in range(1, ny):
        total = total + sel_in[k, 0:slots].astype(F32)
    v_slots[...] = total

    acc = jnp.zeros((blocks, edge), F32)
    for base in range(0, slots, eight):
        left, right = [], []
        for t in range(base, base + eight):
            mine = (first_w <= float(t)) & (last_w > float(t))
            left.append(
                jnp.where(mine, jnp.broadcast_to(v_slots[t : t + 1], (blocks, edge)), 0.0).astype(BF16)
            )
            right.append(tiles[t])
        acc = acc + dot(jnp.concatenate(left, axis=1), jnp.concatenate(right, axis=1), ((1,), (1,)))
    v_own = picked[slots : slots + MB_DEV].astype(BF16).astype(F32)
    owns.wait_recv()
    for k in range(1, ny):
        v_own = v_own + sel_in[k, slots:wide].astype(F32)[0:MB_DEV]

    def over_rows(value):
        return jnp.sum(value, axis=0, keepdims=True)

    x_src[0:blocks] = acc
    terms = [over_rows(v_own * v_own), over_rows(acc * d), over_rows(d * d)]
    x_src[blocks:] = jnp.concatenate(terms + [jnp.zeros((8 - len(terms), edge), F32)], axis=0)
    rows = pl.ds(0, blocks + len(terms))
    for k in far(nx) + [0]:
        for i in range(CORES):
            if k + i > 0:
                send(x_src.at[rows], x_in.at[nx * i + k, rows], s_x, r_x, peer(dx=k, dc=i))
    over_x = group(x_in.at[1 : CORES * nx, rows], s_x, r_x)
    sent.append(over_x)
    over_x.wait_recv()
    own, other = x_src[0 : blocks + 2], x_in[nx, 0 : blocks + 2]
    for k in range(1, nx):
        own = own + x_in[k, 0 : blocks + 2]
        other = other + x_in[nx + k, 0 : blocks + 2]
    g = own[0:blocks]
    g_other = other[0:blocks]
    v_row = own[blocks : blocks + 1] + other[blocks : blocks + 1]
    gd_row = own[blocks + 1 : blocks + 2] + other[blocks + 1 : blocks + 2]
    d_row = x_src[blocks + 2 : blocks + 3] + x_in[nx, blocks + 2 : blocks + 3]
    g_row = over_rows(g * g + g_other * g_other)

    quarter = edge // 4
    stack = jnp.concatenate([g_row, gd_row, d_row, v_row, jnp.zeros((4, edge), F32)], axis=0)
    stack = stack + pltpu.roll(stack, 2 * quarter, 1)
    stack = stack + pltpu.roll(stack, quarter, 1)
    mine = iota((8, edge), 1) // quarter == iota((8, edge), 0)
    f_in[0:1] = over_rows(jnp.where(mine, stack, 0.0))
    for i in far(ny) + [0]:
        for k in far(nz) + [0]:
            slot = i * nz + k
            if slot > 0:
                send(f_in.at[0:1], f_in.at[slot : slot + 1], s_f, r_f, peer(dy=i, dz=k))
    finals = group(f_in.at[1 : ny * nz], s_f, r_f)
    sent.append(finals)
    for stage in sent:
        stage.wait_send()
    finals.wait_recv()
    sums = jnp.broadcast_to(over_rows(f_in[...]), (8, edge))
    sums = jnp.sum(jnp.where(mine, sums, 0.0), axis=1, keepdims=True)
    g_sq, gd, d_sq, v_sq = sums[0:1], sums[1:2], sums[2:3], sums[3:4]
    beta0_sq = d_sq + EPS
    beta0 = jnp.sqrt(beta0_sq)
    alpha_sq = v_sq / beta0_sq + EPS
    alpha = jnp.sqrt(alpha_sq)
    scale = 1.0 / (beta0 * alpha)
    u_sq = g_sq * (scale * scale) - (2.0 / beta0_sq) * gd + (alpha_sq / beta0_sq) * d_sq
    beta_sq = jnp.maximum(u_sq, 0.0) + EPS
    back = 1.0 / jnp.sqrt(beta_sq)
    ray_out[...] = g * (scale * back) - d * (alpha / beta0 * back)
    model_out[...] = v_own * (1.0 / (alpha_sq + beta_sq))


def build(mesh, ny, nz, nx):
    def on_device(tiles, tile_model, ray_counts, data):
        slots, edge = tiles.shape[2], tiles.shape[3]
        blocks = ray_counts.shape[2]
        chunks = 4
        wide = slots + 16
        rows = ny * wide
        integers = jnp.pad(tile_model, ((0, 0), (0, 0), (0, edge - slots))) + jnp.pad(
            ray_counts, ((0, 0), (0, 0), (slots, edge - slots - blocks))
        )
        vmem, dma = pltpu.VMEM, pltpu.SemaphoreType.DMA
        model, rays = pl.pallas_call(
            functools.partial(kernel, ny, nz, nx, slots, blocks, chunks, wide),
            out_shape=(
                jax.ShapeDtypeStruct((MB_DEV, edge), F32),
                jax.ShapeDtypeStruct((blocks, edge), F32),
            ),
            in_specs=[
                pl.BlockSpec(memory_space=pl.ANY),
                pl.BlockSpec(memory_space=pltpu.VMEM),
                pl.BlockSpec(memory_space=pl.ANY),
            ],
            out_specs=(pl.BlockSpec(memory_space=pltpu.VMEM), pl.BlockSpec(memory_space=pltpu.VMEM)),
            scratch_shapes=[
                vmem((slots, edge, edge), BF16),
                vmem((blocks, edge), F32),
                vmem((16, edge), F32),
                vmem((CORES * nz, edge), F32),
                vmem((8, edge), F32),
                vmem((ny, edge), F32),
                vmem((nz // 2, CORES, 2, slots, edge), BF16),
                vmem((nz // 2, rows, CORES * 2 * slots), BF16),
                vmem((rows, edge), F32),
                vmem((ny, wide, edge), BF16),
                vmem((ny, wide, edge), BF16),
                vmem((slots, edge), F32),
                vmem((blocks + 8, edge), F32),
                vmem((CORES * nx, blocks + 8, edge), F32),
                vmem((ny * nz, edge), F32),
                dma((chunks,)), dma,
                dma, dma,
                dma, dma,
                dma((nz // 2,)), dma((nz // 2,)),
                dma, dma((nz // 2,)),
                dma, dma,
                dma, dma,
                dma, dma,
                dma, dma,
            ],
            compiler_params=pltpu.CompilerParams(
                collective_id=0, has_side_effects=True, vmem_limit_bytes=55212 * 1024
            ),
        )(tiles, integers, data.reshape(blocks, edge))
        return model.reshape(1, -1), rays.reshape(-1)

    return jax.shard_map(
        on_device,
        mesh=mesh,
        in_specs=(
            P("row", "col", None, None, None),
            P("row", "col", None),
            P("row", "col", None),
            P("row"),
        ),
        out_specs=(P("col", "row"), P("row")),
        check_vma=False,
    )


def solution(mesh):
    nz = 12
    return build(mesh, mesh.shape["row"] // (CORES * nz), nz, mesh.shape["col"])
```

time: 59.2 us -> 52.9 us (0.89)
  Pallas kernels: 55.8 us -> 50.1 us
  local copies, waits for them, and re-layouts: 2.56 us -> 1.19 us
  other arithmetic: 0 us -> 0.75 us
    pallas_call x1, Pallas kernels: 55.8 us -> 50.1 us  [on_device(): pl.pallas_call(functools.partial(kernel, ny, nz, nx, slots, blocks, chunk...]
    unnamed x2, local copies, waits for them, and re-layouts: 2.56 us -> 1.19 us
    add x0 -> x1, other arithmetic: none -> 0.75 us  [on_device(): jnp.pad(tile_model, ((0, 0), (0, 0), (0, edge - slots)))]
where the time goes in v3:
time: 52.9 us; the launch traced here: 52.7 us
  Pallas kernels  50.1 us (95%)
  local copies, waits for them, and re-layouts  1.19 us (2%)
  other arithmetic  0.75 us (1%)
  between operations  0.64 us (1%)
    pallas_call x1, Pallas kernels, on_device(): pl.pallas_call(functools.partial(kernel, ny, nz, nx, slots, blocks, chunk...  50.1 us
    unnamed x2, local copies, waits for them, and re-layouts  1.19 us

profile of v3, /device:TPU:1, one launch (start us, length us, event | category | flops | bytes accessed | tf_op | source)
XLA Modules:
  0.0 52.7 jit_solution(5051759115288280741)
XLA Ops:
  0.6 0.7 %pad_add_fusion.integers = s32[1,1,128]{2,1,0:T(1,128)S(1)} fusion(s32[1,1,16]{2,1,0:T(1,128)} %param.6, s32[1,1,64]{2,1,0:T(1,128)} %param.5), kind=kLoop, calls=%fused_computation | loop fusion | flops 128 | bytes 832 | tf_op jit(solution)/shard_map/add | solution.py:284
  1.4 50.1 %shard_map.59 = (f32[8,128]{1,0:T(8,128)S(1)}, f32[16,128]{1,0:T(8,128)S(1)}) custom-call(bf16[1,1,64,128,128]{4,3,2,1,0:T(8,128)(2,1)} %tiles_hbm.1, s32[1,1,128]{2,1,0:T(1,128)S(1)} %pad_add_fusion.integers, f32[16,128]{1,0:T(8,128)} %bitcast.5), custom_call_target="tpu_custom_call" | custom-call | tf_op jit(solution)/shard_map/pallas_call | solution.py:288
  51.5 0.6 %copy.8 = f32[1,1024]{1,0:T(1,128)} copy(f32[1,1024]{1,0:T(1,128)S(1)} %bitcast.4) | data formatting | bytes 8192
  52.1 0.6 %copy.9 = f32[2048]{0:T(1024)} copy(f32[2048]{0:T(1024)S(1)} %bitcast.3) | data formatting | bytes 16384

commit v4 on v3

--- a/solution.py
+++ b/solution.py
@@ -25,9 +25,9 @@
 def kernel(
     ny, nz, nx, slots, blocks, chunks, wide,
     tiles_hbm, integers, data_hbm, model_out, ray_out,
-    tiles, data, give_src, give, ask_src, ask, prod, match, picked,
+    tiles, data, give_src, give, give_in, ask_src, ask, prod, match, picked,
     sel_src, sel_in, v_slots, x_src, x_in, f_in,
-    tile_sem, in_sem, s_give, r_give, s_ask, r_ask, s_prod, r_prod, s_rel, r_rel,
+    tile_sem, in_sem, s_give, r_give, s_give2, r_give2, s_ask, r_ask, s_prod, r_prod, s_rel, r_rel,
     s_sel, r_sel, s_own, r_own, s_x, r_x, s_f, r_f,
 ):
     edge = tiles.shape[-1]
@@ -71,7 +71,7 @@
         )
 
     barrier = pltpu.get_barrier_semaphore()
-    greeted = [peer(dz=d, dc=k) for d in far(nz) for k in range(CORES)]
+    greeted = [peer(dz=d) for d in far(nz)]
     greeted += [peer(dy=d) for d in far(ny)]
     greeted += [peer(dx=d, dc=k) for d in far(nx) for k in range(CORES)]
     greeted += [peer(dc=1)]
@@ -132,13 +132,9 @@
     pl.semaphore_wait(barrier, len(greeted))
     for k in far(ny):
         send(ask_src.at[0:1], ask.at[k : k + 1], s_ask, r_ask, peer(dy=k))
-    for k in far(nz) + [0]:
-        for i in range(CORES):
-            if k + i > 0:
-                half, slot = 8 * place[k][1], i * nz + k
-                send(
-                    give_src.at[half : half + 1], give.at[slot : slot + 1], s_give, r_give, peer(dz=k, dc=i)
-                )
+    for k in far(nz):
+        half = 8 * place[k][1]
+        send(give_src.at[half : half + 1], give.at[k : k + 1], s_give, r_give, peer(dz=k))
     for k in far(nz):
         pair, j = place[k]
         send(home, prod.at[pair, 0, j], s_prod.at[pair], r_prod.at[pair], peer(dz=k))
@@ -147,7 +143,7 @@
         for pair in range(nz // 2)
     ]
     asks = group(ask.at[1:ny], s_ask, r_ask)
-    gives = group(give.at[1 : CORES * nz], s_give, r_give)
+    gives = group(give.at[1:nz], s_give, r_give)
     relays = [group(prod.at[pair, 1], s_rel, r_rel.at[pair]) for pair in range(nz // 2)]
     relayed = group(prod.at[:, 0], s_rel, r_rel.at[0])
 
@@ -158,16 +154,20 @@
     relay(0)
     sent += [asks, gives, relayed] + prods
 
+    half = 8 * place[0][1]
+    give[0:1] = give_src[half : half + 1]
+    gives.wait_recv()
+    other_gives = send(give.at[0:nz], give_in, s_give2, r_give2, peer(dc=1))
+    sent.append(other_gives)
     asks.wait_recv()
     ask[0:1] = ask_src[0:1]
     ask_cols = ask[...].T
-    gives.wait_recv()
-    half = 8 * place[0][1]
-    give[0:1] = give_src[half : half + 1]
+    other_gives.wait_recv()
     for pair in range(nz // 2):
         for i in range(CORES):
-            k0, k1 = i * nz + order[2 * pair], i * nz + order[2 * pair + 1]
-            given = jnp.maximum(give[k0 : k0 + 1], give[k1 : k1 + 1])
+            k0, k1 = order[2 * pair], order[2 * pair + 1]
+            table = (give, give_in)[i]
+            given = jnp.maximum(table[k0 : k0 + 1], table[k1 : k1 + 1])
             for p in range(ny):
                 wanted = jnp.broadcast_to(ask_cols[0:wide, p : p + 1], (wide, edge))
                 match[pair, p * wide : (p + 1) * wide, i * edge : (i + 1) * edge] = jnp.where(
@@ -215,8 +215,7 @@
         acc = acc + dot(jnp.concatenate(left, axis=1), jnp.concatenate(right, axis=1), ((1,), (1,)))
     v_own = picked[slots : slots + MB_DEV].astype(BF16).astype(F32)
     owns.wait_recv()
-    for k in range(1, ny):
-        v_own = v_own + sel_in[k, slots:wide].astype(F32)[0:MB_DEV]
+    v_own = v_own + jnp.sum(sel_in[1:ny, slots:wide].astype(F32), axis=0)[0:MB_DEV]
 
     def over_rows(value):
         return jnp.sum(value, axis=0, keepdims=True)
@@ -301,7 +300,8 @@
                 vmem((slots, edge, edge), BF16),
                 vmem((blocks, edge), F32),
                 vmem((16, edge), F32),
-                vmem((CORES * nz, edge), F32),
+                vmem((nz, edge), F32),
+                vmem((nz, edge), F32),
                 vmem((8, edge), F32),
                 vmem((ny, edge), F32),
                 vmem((nz // 2, CORES, 2, slots, edge), BF16),
@@ -314,7 +314,7 @@
                 vmem((CORES * nx, blocks + 8, edge), F32),
                 vmem((ny * nz, edge), F32),
                 dma((chunks,)), dma,
-                dma, dma,
+                dma, dma, dma, dma,
                 dma, dma,
                 dma((nz // 2,)), dma((nz // 2,)),
                 dma, dma((nz // 2,)),

time: 52.9 us -> 52 us (0.983)
  Pallas kernels: 50.1 us -> 49.3 us
    pallas_call x1, Pallas kernels: 50.1 us -> 49.3 us  [on_device(): pl.pallas_call(functools.partial(kernel, ny, nz, nx, slots, blocks, chunk...]
where the time goes in v4:
time: 52 us; the launch traced here: 51.9 us
  Pallas kernels  49.3 us (95%)
  local copies, waits for them, and re-layouts  1.19 us (2%)
  other arithmetic  0.75 us (1%)
  between operations  0.64 us (1%)
    pallas_call x1, Pallas kernels, on_device(): pl.pallas_call(functools.partial(kernel, ny, nz, nx, slots, blocks, chunk...  49.3 us
    unnamed x2, local copies, waits for them, and re-layouts  1.19 us

profile of v4, /device:TPU:1, one launch (start us, length us, event | category | flops | bytes accessed | tf_op | source)
XLA Modules:
  0.0 51.9 jit_solution(1561989980750137898)
XLA Ops:
  0.6 0.7 %pad_add_fusion.integers = s32[1,1,128]{2,1,0:T(1,128)S(1)} fusion(s32[1,1,16]{2,1,0:T(1,128)} %param.6, s32[1,1,64]{2,1,0:T(1,128)} %param.5), kind=kLoop, calls=%fused_computation | loop fusion | flops 128 | bytes 832 | tf_op jit(solution)/shard_map/add | solution.py:283
  1.4 49.3 %shard_map.59 = (f32[8,128]{1,0:T(8,128)S(1)}, f32[16,128]{1,0:T(8,128)S(1)}) custom-call(bf16[1,1,64,128,128]{4,3,2,1,0:T(8,128)(2,1)} %tiles_hbm.1, s32[1,1,128]{2,1,0:T(1,128)S(1)} %pad_add_fusion.integers, f32[16,128]{1,0:T(8,128)} %bitcast.5), custom_call_target="tpu_custom_call" | custom-call | tf_op jit(solution)/shard_map/pallas_call | solution.py:287
  50.7 0.6 %copy.8 = f32[1,1024]{1,0:T(1,128)} copy(f32[1,1024]{1,0:T(1,128)S(1)} %bitcast.4) | data formatting | bytes 8192
  51.3 0.6 %copy.9 = f32[2048]{0:T(1024)} copy(f32[2048]{0:T(1024)S(1)} %bitcast.3) | data formatting | bytes 16384

commit v5 on v4

--- a/solution.py
+++ b/solution.py
@@ -25,7 +25,7 @@
 def kernel(
     ny, nz, nx, slots, blocks, chunks, wide,
     tiles_hbm, integers, data_hbm, model_out, ray_out,
-    tiles, data, give_src, give, give_in, ask_src, ask, prod, match, picked,
+    tiles, turned, data, give_src, give, give_in, ask_src, ask, prod, match, picked,
     sel_src, sel_in, v_slots, x_src, x_in, f_in,
     tile_sem, in_sem, s_give, r_give, s_give2, r_give2, s_ask, r_ask, s_prod, r_prod, s_rel, r_rel,
     s_sel, r_sel, s_own, r_own, s_x, r_x, s_f, r_f,
@@ -53,6 +53,19 @@
         )
         copy.start()
         return copy
+
+    def group(ref, s_sem, r_sem):
+        return pltpu.make_async_remote_copy(
+            src_ref=ref, dst_ref=ref, send_sem=s_sem, recv_sem=r_sem, device_id=peer(dc=1), device_id_type=MESH
+        )
+
+    barrier = pltpu.get_barrier_semaphore()
+    greeted = [peer(dz=d) for d in far(nz)]
+    greeted += [peer(dy=d) for d in far(ny)]
+    greeted += [peer(dx=d, dc=k) for d in far(nx) for k in range(CORES)]
+    greeted += [peer(dc=1)]
+    for target in greeted:
+        pl.semaphore_signal(barrier, inc=1, device_id=target, device_id_type=MESH)
 
     data_load = pltpu.make_async_copy(data_hbm, data, in_sem)
     data_load.start()
@@ -64,19 +77,6 @@
         )
         load.start()
         loads.append(load)
-
-    def group(ref, s_sem, r_sem):
-        return pltpu.make_async_remote_copy(
-            src_ref=ref, dst_ref=ref, send_sem=s_sem, recv_sem=r_sem, device_id=peer(dc=1), device_id_type=MESH
-        )
-
-    barrier = pltpu.get_barrier_semaphore()
-    greeted = [peer(dz=d) for d in far(nz)]
-    greeted += [peer(dy=d) for d in far(ny)]
-    greeted += [peer(dx=d, dc=k) for d in far(nx) for k in range(CORES)]
-    greeted += [peer(dc=1)]
-    for target in greeted:
-        pl.semaphore_signal(barrier, inc=1, device_id=target, device_id_type=MESH)
 
     count_row = integers[0].astype(F32)[:, slots : slots + blocks]
     count_all = jnp.broadcast_to(count_row, (blocks, blocks))
@@ -154,11 +154,22 @@
     relay(0)
     sent += [asks, gives, relayed] + prods
 
+    for t in range(slots):
+        turned[t] = tiles[t].T
     half = 8 * place[0][1]
     give[0:1] = give_src[half : half + 1]
     gives.wait_recv()
     other_gives = send(give.at[0:nz], give_in, s_give2, r_give2, peer(dc=1))
     sent.append(other_gives)
+    per = nz // 4
+
+    def fetch(part):
+        for pair in range(part * per, (part + 1) * per):
+            prods[pair].wait_recv()
+            for k in order[2 * pair : 2 * pair + 2]:
+                if k > 0:
+                    relay(k)
+
     asks.wait_recv()
     ask[0:1] = ask_src[0:1]
     ask_cols = ask[...].T
@@ -167,26 +178,25 @@
         for i in range(CORES):
             k0, k1 = order[2 * pair], order[2 * pair + 1]
             table = (give, give_in)[i]
+            part, lanes = pair // per, (pair % per * CORES + i) * edge
             given = jnp.maximum(table[k0 : k0 + 1], table[k1 : k1 + 1])
             for p in range(ny):
                 wanted = jnp.broadcast_to(ask_cols[0:wide, p : p + 1], (wide, edge))
-                match[pair, p * wide : (p + 1) * wide, i * edge : (i + 1) * edge] = jnp.where(
+                match[part, p * wide : (p + 1) * wide, lanes : lanes + edge] = jnp.where(
                     wanted == given, 1.0, 0.0
                 ).astype(BF16)
 
-    def add(pair):
-        relays[pair].wait_recv()
-        part = dot(match[pair], prod[pair].reshape(CORES * 2 * slots, edge))
-        picked[...] = part if pair == 0 else picked[...] + part
-
-    for pair in range(nz // 2):
-        prods[pair].wait_recv()
-        for k in order[2 * pair : 2 * pair + 2]:
-            if k > 0:
-                relay(k)
-        if pair > 0:
-            add(pair - 1)
-    add(nz // 2 - 1)
+    def add(part):
+        pairs = slice(part * per, (part + 1) * per)
+        for pair in range(part * per, (part + 1) * per):
+            relays[pair].wait_recv()
+        found = dot(match[part], prod[pairs].reshape(per * CORES * 2 * slots, edge))
+        picked[...] = found if part == 0 else picked[...] + found
+
+    fetch(0)
+    fetch(1)
+    add(0)
+    add(1)
 
     sel_src[...] = picked[...].astype(BF16).reshape(ny, wide, edge)
     slot_rows, own_rows = pl.ds(0, slots), pl.ds(slots, wide - slots)
@@ -205,14 +215,13 @@
 
     acc = jnp.zeros((blocks, edge), F32)
     for base in range(0, slots, eight):
-        left, right = [], []
+        left = []
         for t in range(base, base + eight):
             mine = (first_w <= float(t)) & (last_w > float(t))
             left.append(
                 jnp.where(mine, jnp.broadcast_to(v_slots[t : t + 1], (blocks, edge)), 0.0).astype(BF16)
             )
-            right.append(tiles[t])
-        acc = acc + dot(jnp.concatenate(left, axis=1), jnp.concatenate(right, axis=1), ((1,), (1,)))
+        acc = acc + dot(jnp.concatenate(left, axis=1), turned[base : base + eight].reshape(eight * edge, edge))
     v_own = picked[slots : slots + MB_DEV].astype(BF16).astype(F32)
     owns.wait_recv()
     v_own = v_own + jnp.sum(sel_in[1:ny, slots:wide].astype(F32), axis=0)[0:MB_DEV]
@@ -298,6 +307,7 @@
             out_specs=(pl.BlockSpec(memory_space=pltpu.VMEM), pl.BlockSpec(memory_space=pltpu.VMEM)),
             scratch_shapes=[
                 vmem((slots, edge, edge), BF16),
+                vmem((slots, edge, edge), BF16),
                 vmem((blocks, edge), F32),
                 vmem((16, edge), F32),
                 vmem((nz, edge), F32),
@@ -305,7 +315,7 @@
                 vmem((8, edge), F32),
                 vmem((ny, edge), F32),
                 vmem((nz // 2, CORES, 2, slots, edge), BF16),
-                vmem((nz // 2, rows, CORES * 2 * slots), BF16),
+                vmem((2, rows, nz // 2 * CORES * slots), BF16),
                 vmem((rows, edge), F32),
                 vmem((ny, wide, edge), BF16),
                 vmem((ny, wide, edge), BF16),

time: 52 us -> 50.5 us (0.971)
  Pallas kernels: 49.3 us -> 47.7 us
    pallas_call x1, Pallas kernels: 49.3 us -> 47.7 us  [on_device(): pl.pallas_call(functools.partial(kernel, ny, nz, nx, slots, blocks, chunk...]
where the time goes in v5:
time: 50.5 us; the launch traced here: 50.3 us
  Pallas kernels  47.7 us (94%)
  local copies, waits for them, and re-layouts  1.19 us (2%)
  other arithmetic  0.75 us (1%)
  between operations  0.64 us (1%)
    pallas_call x1, Pallas kernels, on_device(): pl.pallas_call(functools.partial(kernel, ny, nz, nx, slots, blocks, chunk...  47.7 us
    unnamed x2, local copies, waits for them, and re-layouts  1.19 us

profile of v5, /device:TPU:1, one launch (start us, length us, event | category | flops | bytes accessed | tf_op | source)
XLA Modules:
  0.0 50.3 jit_solution(12617844850398052966)
XLA Ops:
  0.6 0.7 %pad_add_fusion.integers = s32[1,1,128]{2,1,0:T(1,128)S(1)} fusion(s32[1,1,16]{2,1,0:T(1,128)} %param.6, s32[1,1,64]{2,1,0:T(1,128)} %param.5), kind=kLoop, calls=%fused_computation | loop fusion | flops 128 | bytes 832 | tf_op jit(solution)/shard_map/add | solution.py:292
  1.4 47.7 %shard_map.59 = (f32[8,128]{1,0:T(8,128)S(1)}, f32[16,128]{1,0:T(8,128)S(1)}) custom-call(bf16[1,1,64,128,128]{4,3,2,1,0:T(8,128)(2,1)} %tiles_hbm.1, s32[1,1,128]{2,1,0:T(1,128)S(1)} %pad_add_fusion.integers, f32[16,128]{1,0:T(8,128)} %bitcast.5), custom_call_target="tpu_custom_call" | custom-call | tf_op jit(solution)/shard_map/pallas_call | solution.py:296
  49.1 0.6 %copy.8 = f32[1,1024]{1,0:T(1,128)} copy(f32[1,1024]{1,0:T(1,128)S(1)} %bitcast.4) | data formatting | bytes 8192
  49.7 0.6 %copy.9 = f32[2048]{0:T(1024)} copy(f32[2048]{0:T(1024)S(1)} %bitcast.3) | data formatting | bytes 16384

commit v6 on v5

--- a/solution.py
+++ b/solution.py
@@ -178,7 +178,7 @@
         for i in range(CORES):
             k0, k1 = order[2 * pair], order[2 * pair + 1]
             table = (give, give_in)[i]
-            part, lanes = pair // per, (pair % per * CORES + i) * edge
+            part, lanes = i, pair * edge
             given = jnp.maximum(table[k0 : k0 + 1], table[k1 : k1 + 1])
             for p in range(ny):
                 wanted = jnp.broadcast_to(ask_cols[0:wide, p : p + 1], (wide, edge))
@@ -187,15 +187,14 @@
                 ).astype(BF16)
 
     def add(part):
-        pairs = slice(part * per, (part + 1) * per)
-        for pair in range(part * per, (part + 1) * per):
-            relays[pair].wait_recv()
-        found = dot(match[part], prod[pairs].reshape(per * CORES * 2 * slots, edge))
+        found = dot(match[part], prod[:, part].reshape(nz * slots, edge))
         picked[...] = found if part == 0 else picked[...] + found
 
     fetch(0)
     fetch(1)
     add(0)
+    for pair in range(nz // 2):
+        relays[pair].wait_recv()
     add(1)
 
     sel_src[...] = picked[...].astype(BF16).reshape(ny, wide, edge)

time: 50.5 us -> 50.4 us (level)
  no operation moved by 1% of the time
where the time goes in v6:
time: 50.4 us; the launch traced here: 50.3 us
  Pallas kernels  47.7 us (95%)
  local copies, waits for them, and re-layouts  1.19 us (2%)
  other arithmetic  0.75 us (1%)
  between operations  0.64 us (1%)
    pallas_call x1, Pallas kernels, on_device(): pl.pallas_call(functools.partial(kernel, ny, nz, nx, slots, blocks, chunk...  47.7 us
    unnamed x2, local copies, waits for them, and re-layouts  1.19 us

profile of v6, /device:TPU:1, one launch (start us, length us, event | category | flops | bytes accessed | tf_op | source)
XLA Modules:
  0.0 50.3 jit_solution(10879688516162368530)
XLA Ops:
  0.6 0.7 %pad_add_fusion.integers = s32[1,1,128]{2,1,0:T(1,128)S(1)} fusion(s32[1,1,16]{2,1,0:T(1,128)} %param.6, s32[1,1,64]{2,1,0:T(1,128)} %param.5), kind=kLoop, calls=%fused_computation | loop fusion | flops 128 | bytes 832 | tf_op jit(solution)/shard_map/add | solution.py:291
  1.4 47.7 %shard_map.59 = (f32[8,128]{1,0:T(8,128)S(1)}, f32[16,128]{1,0:T(8,128)S(1)}) custom-call(bf16[1,1,64,128,128]{4,3,2,1,0:T(8,128)(2,1)} %tiles_hbm.1, s32[1,1,128]{2,1,0:T(1,128)S(1)} %pad_add_fusion.integers, f32[16,128]{1,0:T(8,128)} %bitcast.5), custom_call_target="tpu_custom_call" | custom-call | tf_op jit(solution)/shard_map/pallas_call | solution.py:295
  49.1 0.6 %copy.8 = f32[1,1024]{1,0:T(1,128)} copy(f32[1,1024]{1,0:T(1,128)S(1)} %bitcast.4) | data formatting | bytes 8192
  49.7 0.6 %copy.9 = f32[2048]{0:T(1024)} copy(f32[2048]{0:T(1024)S(1)} %bitcast.3) | data formatting | bytes 16384
